TPU v7x, 128 devices: a whole 4x4x4 slice. The times are simulated.
128 devices in a mesh: grp: 4 (over x), gx: 4 (over z_lo, core), gy: 8 (over z_hi, y).
Axes of the slice: x: 4, y: 4, z: 4 (z_hi: 2, z_lo: 2; z = z_hi * 2 + z_lo), core: 2. Of those that a mesh axis runs over, the one named last changes fastest.
Arguments:
- flow_state: float32 [8, 768, 128, 128], P(None, ('grp', 'gx'), 'gy'), may hold values from -90 to 90
- speeds: float32 [3, 8], replicated, may hold values from 0.3 to 1.2
- viscosity: float32 [8], replicated, may hold values from 0.02 to 0.2
- reaction: float32 [8, 8], replicated, may hold values from -2 to 2
- start_basis: float32 [768, 96], replicated, may hold values from -6 to 6
- slab_table: int32 [8, 8, 1], replicated, may hold values from 0 to 15; in each aligned block of 8 rows (0 to 7, 8 to 15, ..., all dimensions but the last counted through in order) at most 2 rows name the same one
Outputs:
- final_state: float32 [8, 768, 128, 128], P(None, ('grp', 'gx'), 'gy')
- core_slots: float32 [256, 96, 8, 2, 128], P(('grp', 'gx', 'gy'))
Inputs may be any that keep to these rules, and one draw needn't show every extreme that they name: slab_table[t, u, 0] names the slab that stores unit u of row t; within each row t no slab is named by more than 2 units, a bound that some block reaches.
All inputs are finite; a program needn't handle non-finite values.
Results may differ from a plain program's by a relative error of at most 0.0034.
Values may be sent and summed in bfloat16 or wider, within the bound.
A program may use at most 256 MiB of HBM per device.

v0:
```python
import jax
import jax.numpy as jnp
from jax import lax
from jax.sharding import PartitionSpec as P

V = 8
NX = 768
R = 96
NZ = 128
YB = 2
NEWTON = 5
slope_weights = (0.8, -0.2, 4.0 / 105.0, -1.0 / 280.0)
curve_weights = (1.6, -0.2, 8.0 / 315.0, -1.0 / 560.0)
curve_center = -205.0 / 72.0
time_step = 0.2


def extended(shard, sides, width):
    for axis, dim in sides:
        peers, length = (lax.axis_size(axis), shard.shape[dim])
        up = [(i, (i + 1) % peers) for i in range(peers)]
        down = [(j, i) for i, j in up]
        last = lax.slice_in_dim(shard, length - width, length, axis=dim)
        initial = lax.slice_in_dim(shard, 0, width, axis=dim)
        before = lax.ppermute(last, axis, up)
        after = lax.ppermute(initial, axis, down)
        shard = jnp.concatenate([before, shard, after], axis=dim)
    return shard


def tendency(padded, speeds, viscosity, reaction):
    center = padded[:, 4:-4, 4:-4, :]
    width_first = center.shape[1]
    width_second = center.shape[2]
    diffusion = viscosity[:, None, None, None]
    speed_one = speeds[0][:, None, None, None]
    speed_two = speeds[1][:, None, None, None]
    speed_three = speeds[2][:, None, None, None]
    summed = 3.0 * curve_center * diffusion * center
    summed = summed + jnp.einsum("kj,jxyz->kxyz", reaction, center, precision=lax.Precision.HIGHEST)
    for offset in range(1, 5):
        slope_weight = slope_weights[offset - 1]
        curve_weight = curve_weights[offset - 1]
        spread = curve_weight * diffusion
        summed = summed + (
            (spread - slope_weight * speed_one)
            * padded[:, 4 + offset : 4 + offset + width_first, 4 : 4 + width_second, :]
            + (spread + slope_weight * speed_one)
            * padded[:, 4 - offset : 4 - offset + width_first, 4 : 4 + width_second, :]
            + (spread - slope_weight * speed_two)
            * padded[:, 4 : 4 + width_first, 4 + offset : 4 + offset + width_second, :]
            + (spread + slope_weight * speed_two)
            * padded[:, 4 : 4 + width_first, 4 - offset : 4 - offset + width_second, :]
            + (spread - slope_weight * speed_three) * jnp.roll(center, -offset, 3)
            + (spread + slope_weight * speed_three) * jnp.roll(center, offset, 3)
        )
    return summed


def extend(field):
    return extended(field, ((("grp", "gx"), 1), ("gy", 2)), 4)


def on_device(flow_state, speeds, viscosity, reaction, start_basis, slab_table):
    first = flow_state + time_step * tendency(extend(flow_state), speeds, viscosity, reaction)
    final_state = 0.5 * flow_state + 0.5 * (
        first + time_step * tendency(extend(first), speeds, viscosity, reaction)
    )
    snapshot = final_state.astype(jnp.bfloat16)
    tile_rows = flow_state.shape[1]
    unit_count = flow_state.shape[2] // YB
    slab_count = lax.axis_size(("grp", "gx"))
    capacity = max(2, 3 * unit_count // slab_count)
    columns = V * YB * NZ
    table_row = lax.dynamic_index_in_dim(
        slab_table[:, :, 0], lax.axis_index("gy"), 0, keepdims=False
    )
    order = jnp.arange(unit_count, dtype=jnp.int32)
    earlier = order[None, :] < order[:, None]
    same_slab = table_row[:, None] == table_row[None, :]
    slot_index = jnp.sum((same_slab & earlier).astype(jnp.int32), axis=1)
    target = table_row * capacity + slot_index
    placing = (
        jnp.arange(slab_count * capacity, dtype=jnp.int32)[:, None] == target[None, :]
    ).astype(jnp.bfloat16)
    blocks = snapshot.reshape(V, tile_rows, unit_count, YB, NZ)
    outgoing = jnp.einsum(
        "pu,vxuyz->pxvyz", placing, blocks, preferred_element_type=jnp.float32
    ).astype(jnp.bfloat16)
    received = lax.all_to_all(
        outgoing.reshape(slab_count, capacity, tile_rows, columns),
        ("grp", "gx"),
        split_axis=0,
        concat_axis=2,
        tiled=True,
    )
    received = received.reshape(capacity, NX, columns)
    partial_value = lax.dot_general(
        received, received, (((0, 2), (0, 2)), ((), ())), preferred_element_type=jnp.float32
    )
    gram = lax.psum(partial_value, ("grp", "gx", "gy"))
    product = jnp.dot(gram, start_basis, precision=lax.Precision.HIGHEST)
    basis = product / jnp.sqrt(jnp.sum(product * product))
    for repeat in range(NEWTON):
        inner_gram = jnp.dot(basis.T, basis, precision=lax.Precision.HIGHEST)
        basis = 1.5 * basis - 0.5 * jnp.dot(basis, inner_gram, precision=lax.Precision.HIGHEST)
    basis_half = basis.astype(jnp.bfloat16)
    cores = jnp.einsum("xr,mxc->mrc", basis_half, received, preferred_element_type=jnp.float32)
    return (final_state, cores.reshape(capacity, R, V, YB, NZ))


def solution(mesh):
    placed = (P(None, ("grp", "gx"), "gy", None), P(), P(), P(), P(), P())
    return jax.shard_map(
        on_device,
        mesh=mesh,
        in_specs=placed,
        out_specs=(
            P(None, ("grp", "gx"), "gy", None),
            P(("grp", "gx", "gy"), None, None, None, None),
        ),
        check_vma=False,
    )
```

profile of v0, /device:TPU:1, one launch (start us, length us, event | category | flops | bytes accessed | tf_op | source)
XLA Modules:
  0.0 518.8 jit_solution(14506563445527793642)
XLA Ops:
  7.2 1.1 fusion.116
  8.3 0.9 copy.103
  9.2 3.0 collective-permute-start.1
  12.2 0.9 copy.104
  13.1 5.8 %fusion.114 = (f32[8,48,16,1]{3,2,1,0:T(8,128)S(1)}, f32[8,48,16,1]{3,2,1,0:T(8,128)}) fusion(f32[8,48,16,128]{3,2,1,0:T(8,128)} %param.6), kind=kLoop, calls=%fused_computation.230 | loop fusion | bytes 98304 | tf_op jit(solution)/shard_map/jit(_roll_static)/slice | solution.py:55
  18.9 3.9 fusion.115
  22.7 1.1 fusion.112
  23.8 3.7 fusion.113
  27.5 1.1 fusion.110
  28.6 1.1 fusion.111
  29.7 1.1 fusion.108
  30.8 1.8 constant_dynamic-update-slice_fusion.3
  32.6 5.7 %constant_dynamic-update-slice_fusion.1 = (f32[8,52,16,128]{3,0,2,1:T(8,128)}, f32[8,52,16,128]{3,0,2,1:T(8,128)}, f32[8,56,16,128]{3,0,2,1:T(8,128)}) fusion(f32[8,48,16,128]{3,2,1,0:T(8,128)S(1)} %copy-done.1, f32[8,52,16,128]{3,0,2,1:T(8,128)} %get-tuple-element.55, f32[8,56,16,128]{3,0,2,1:T(8,128)} %get-tuple-element.56), kind=kLoop, calls=%fused_computation.168 | loop fusion | bytes 12582912
  38.3 0.8 constant_dynamic-update-slice_fusion
  39.2 2.9 fusion.98
  42.0 5.8 %collective-permute-start.2 = (f32[8,56,4,128]{3,0,2,1:T(8,128)}, f32[8,56,4,128]{3,0,2,1:T(8,128)}, u32[]{:S(2)}, u32[]{:S(2)}) collective-permute-start(f32[8,56,4,128]{3,0,2,1:T(8,128)} %get-tuple-element.12), channel_id=1, source_target_pairs={{1,0},{2,1},{3,2},{4,3},{5,4},{6,5},{7,6},{0,7},{9,8},{10,9},{11,1... | collective-permute-start | bytes 2752520 | tf_op jit(solution)/shard_map/ppermute | solution.py:26
  47.9 3.8 fusion.109
  51.7 5.6 %copy.105 = f32[8,48,16,1]{3,0,2,1:T(8,128)} copy(f32[8,48,16,1]{3,2,1,0:T(8,128)} %get-tuple-element.45) | data formatting | bytes 49152
  57.3 3.5 copy.106
  60.8 3.5 copy.107
  64.3 3.5 copy.108
  67.8 3.5 copy.109
  71.4 3.7 copy.110
  75.1 3.4 copy.111
  78.5 3.5 copy.112
  82.0 3.5 copy.113
  85.4 3.4 copy.114
  88.9 3.5 copy.115
  92.4 3.8 copy.116
  96.2 3.5 copy.117
  99.8 3.4 copy.118
  103.2 3.5 copy.119
  106.7 3.4 copy.120
  110.1 0.7 dynamic-slice_bitcast_fusion
  111.0 0.7 multiply_add_fusion
  111.7 37.7 %fusion.43 = f32[8,48,16,128]{3,0,2,1:T(8,128)S(1)} fusion(f32[8,56,16,128]{3,0,2,1:T(8,128)} %get-tuple-element.54, f32[8,56,4,128]{3,0,2,1:T(8,128)} %collective-permute-done.3, f32[8,56,4,128]{3,0,2,1:T(8,128)} %collective-permute-done.2, f32[8,52,16,128]{3,0,2,1:T(8,128)} %get-tuple-element.49, f32[8,52,16,128]{3,0,2,1:T(8,128)} %get-tuple-element.53, ...), kind=kOutput, calls=%fused_computation.70 | convolution fusion | flops 128974848 | bytes 90440736 | tf_op jit(solution)/shard_map/kj,jxyz->kxyz/dot_general | solution.py:40
  149.5 3.8 fusion.99
  153.3 3.8 fusion.100
  157.1 3.8 fusion.101
  161.0 3.9 fusion.102
  164.9 3.8 fusion.103
  168.6 2.8 collective-permute-start.4
  171.4 3.9 fusion.104
  175.3 2.1 collective-permute-done.5
  177.6 5.4 %collective-permute-start.6 = (f32[8,56,4,128]{3,0,2,1:T(8,128)S(1)}, f32[8,56,4,128]{3,0,2,1:T(8,128)S(1)}, u32[]{:S(2)}, u32[]{:S(2)}) collective-permute-start(f32[8,56,4,128]{3,0,2,1:T(8,128)S(1)} %get-tuple-element.10), channel_id=1, source_target_pairs={{1,0},{2,1},{3,2},{4,3},{5,4},{6,5},{7,6},{0,7},{9,8},{10,9},{11,1... | collective-permute-start | bytes 2752520 | tf_op jit(solution)/shard_map/ppermute | solution.py:26
  183.2 3.7 fusion.105
  187.0 3.9 fusion.106
  190.8 9.9 %collective-permute-done.6 = f32[8,56,4,128]{3,0,2,1:T(8,128)S(1)} collective-permute-done((f32[8,56,4,128]{3,0,2,1:T(8,128)S(1)}, f32[8,56,4,128]{3,0,2,1:T(8,128)S(1)}, u32[]{:S(2)}, u32[]{:S(2)}) %collective-permute-start.6) | collective-permute-done | bytes 917536 | tf_op jit(solution)/shard_map/ppermute | solution.py:26
  200.8 5.7 %collective-permute-done.7 = f32[8,56,4,128]{3,0,2,1:T(8,128)S(1)} collective-permute-done((f32[8,56,4,128]{3,0,2,1:T(8,128)S(1)}, f32[8,56,4,128]{3,0,2,1:T(8,128)S(1)}, u32[]{:S(2)}, u32[]{:S(2)}) %collective-permute-start.7) | collective-permute-done | bytes 917536 | tf_op jit(solution)/shard_map/ppermute | solution.py:25
  206.5 3.9 pad_maximum_fusion
  210.4 25.6 %fusion.117 = (bf16[8,48,16,128]{3,0,2,1:T(8,128)(2,1)S(1)}, f32[8,48,16,128]{3,0,2,1:T(8,128)}) fusion(f32[8,48,16,128]{3,0,2,1:T(8,128)S(1)} %fusion.43, f32[8,48,16,124]{3,0,2,1:T(8,128)} %get-tuple-element.16, f32[8,48,16,4]{3,0,2,1:T(8,128)} %get-tuple-element.14, f32[8]{0:T(128)S(1)} %get-tuple-element.62, f32[8,48,16,4]{3,0,2,1:T(8,128)} %get-tuple-element.15, ...), kind=kOutput, calls=%fused_computation.233 | convolution fusion | flops 131334144 | bytes 65028608 | tf_op jit(solution)/shard_map/kj,jxyz->kxyz/dot_general | solution.py:40
  236.0 1.9 convert_bitcast_fusion
  237.9 10.6 %copy.90 = bf16[32,48,8,2,128]{4,3,2,1,0:T(2,128)(2,1)} copy(bf16[32,48,8,2,128]{4,0,3,1,2:T(8,128)(2,1)S(1)} %convert_bitcast_fusion) | data formatting | bytes 12582912 | tf_op jit(solution)/shard_map/convert_element_type | solution.py:89
  248.6 11.1 %reshape.133 = bf16[16,2,48,2048]{3,2,1,0:T(8,128)(2,1)} reshape(bf16[32,48,8,2,128]{4,3,2,1,0:T(2,128)(2,1)} %copy.90) | data formatting | bytes 12582912 | tf_op jit(solution)/shard_map/reshape | solution.py:91
  259.7 78.8 %all_to_all.15 = bf16[16,2,48,2048]{3,2,1,0:T(8,128)(2,1)S(1)} all-to-all(bf16[16,2,48,2048]{3,2,1,0:T(8,128)(2,1)} %reshape.133), channel_id=1, replica_groups=mesh['grp'=4,'gx'=4,'gy'=8] {'grp','gx'}, dimensions={0} | all-to-all | bytes 12582912 | tf_op jit(solution)/shard_map/all_to_all | solution.py:90
  338.5 1.1 copy.91
  339.6 2.7 copy-done.3
  342.3 6.5 %convolution_bitcast_fusion.1 = f32[768,768]{1,0:T(8,128)} fusion(bf16[2,768,2048]{2,1,0:T(8,128)(2,1)S(1)} %bitcast.95), kind=kOutput, calls=%fused_computation.147 | convolution fusion | flops 4831838208 | bytes 8650752 | tf_op jit(solution)/shard_map/dot_general | solution.py:98
  348.8 2.2 copy.92
  351.0 144.7 %all-reduce.2.cloned.1.call-done = f32[768,768]{1,0:T(8,128)} async-done(((f32[768,768]{1,0:T(8,128)}), f32[768,768]{1,0:T(8,128)}) %all-reduce.2.cloned.1.call-update) | async-done | bytes 2359312 | tf_op jit(solution)/shard_map/psum | solution.py:101
  495.8 4.6 multiply_reduce_fusion
  502.3 0.5 fusion.86
  505.4 4.0 convolution_bitcast_fusion
  509.4 2.5 reshape.135
  (56 shorter events, 4.7 us)
Async XLA Ops:
  7.2 488.6 %copy-start = (f32[768,96]{0,1:T(8,128)S(1)}, f32[768,96]{0,1:T(8,128)}, u32[]{:S(2)}) copy-start(f32[768,96]{0,1:T(8,128)} %param.10) | copy-start | bytes 884740
  7.2 488.6 %all-reduce.2.cloned.1.call-start = ((), (), s32[]{:S(2)}) async-start(), calls=%async_computation.1 | async-start | bytes 4718592 | tf_op jit(solution)/shard_map/psum | solution.py:101
  9.2 21.6 %collective-permute-start.1 = (f32[8,4,16,128]{3,0,2,1:T(8,128)}, f32[8,4,16,128]{3,0,2,1:T(8,128)}, u32[]{:S(2)}, u32[]{:S(2)}) collective-permute-start(f32[8,4,16,128]{3,0,2,1:T(8,128)} %copy.103), channel_id=1, source_target_pairs={{0,8},{8,16},{16,24},{24,32},{32,40},{40,48},{48,56},{56,64},{64,7... | collective-permute-start | bytes 786440 | tf_op jit(solution)/shard_map/ppermute | solution.py:25
  13.1 5.8 %copy-start.1 = (f32[8,48,16,128]{3,2,1,0:T(8,128)S(1)}, f32[8,48,16,128]{3,2,1,0:T(8,128)}, u32[]{:S(2)}) copy-start(f32[8,48,16,128]{3,2,1,0:T(8,128)} %param.6) | copy-start | bytes 9437188
  13.1 25.2 %collective-permute-start = (f32[8,4,16,128]{3,0,2,1:T(8,128)}, f32[8,4,16,128]{3,0,2,1:T(8,128)S(1)}, u32[]{:S(2)}, u32[]{:S(2)}) collective-permute-start(f32[8,4,16,128]{3,0,2,1:T(8,128)} %copy.104), channel_id=1, source_target_pairs={{8,0},{16,8},{24,16},{32,24},{40,32},{48,40},{56,48},{64,56},{72,6... | collective-permute-start | bytes 786440 | tf_op jit(solution)/shard_map/ppermute | solution.py:26
  42.0 69.7 %collective-permute-start.2 = (f32[8,56,4,128]{3,0,2,1:T(8,128)}, f32[8,56,4,128]{3,0,2,1:T(8,128)}, u32[]{:S(2)}, u32[]{:S(2)}) collective-permute-start(f32[8,56,4,128]{3,0,2,1:T(8,128)} %get-tuple-element.12), channel_id=1, source_target_pairs={{1,0},{2,1},{3,2},{4,3},{5,4},{6,5},{7,6},{0,7},{9,8},{10,9},{11,1... | collective-permute-start | bytes 2752520 | tf_op jit(solution)/shard_map/ppermute | solution.py:26
  47.8 63.9 %collective-permute-start.3 = (f32[8,56,4,128]{3,0,2,1:T(8,128)}, f32[8,56,4,128]{3,0,2,1:T(8,128)}, u32[]{:S(2)}, u32[]{:S(2)}) collective-permute-start(f32[8,56,4,128]{3,0,2,1:T(8,128)} %get-tuple-element.13), channel_id=1, source_target_pairs={{0,1},{1,2},{2,3},{3,4},{4,5},{5,6},{6,7},{7,0},{8,9},{9,10},{10,1... | collective-permute-start | bytes 2752520 | tf_op jit(solution)/shard_map/ppermute | solution.py:25
  51.7 5.6 %copy-start.7 = (f32[8,48,16,127]{3,2,1,0:T(8,128)S(1)}, f32[8,48,16,127]{3,2,1,0:T(8,128)}, u32[]{:S(2)}) copy-start(f32[8,48,16,127]{3,2,1,0:T(8,128)} %get-tuple-element.47) | copy-start | bytes 9363460
  57.3 3.5 copy-start.6
  67.8 3.6 copy-start.5
  71.4 3.7 copy-start.4
  96.2 3.5 copy-start.9
  99.7 3.4 copy-start.8
  106.7 4.9 copy-start.13
  106.7 4.9 copy-start.14
  106.7 5.0 copy-start.15
  168.6 6.6 %collective-permute-start.4 = (f32[8,4,16,128]{3,0,2,1:T(8,128)S(1)}, f32[8,4,16,128]{3,0,2,1:T(8,128)S(1)}, u32[]{:S(2)}, u32[]{:S(2)}) collective-permute-start(f32[8,4,16,128]{3,0,2,1:T(8,128)S(1)} %get-tuple-element.30), channel_id=1, source_target_pairs={{8,0},{16,8},{24,16},{32,24},{40,32},{48,40},{56,48},{64,56},{72,6... | collective-permute-start | bytes 786440 | tf_op jit(solution)/shard_map/ppermute | solution.py:26
  171.4 6.0 %collective-permute-start.5 = (f32[8,4,16,128]{3,0,2,1:T(8,128)S(1)}, f32[8,4,16,128]{3,0,2,1:T(8,128)S(1)}, u32[]{:S(2)}, u32[]{:S(2)}) collective-permute-start(f32[8,4,16,128]{3,0,2,1:T(8,128)S(1)} %get-tuple-element.31), channel_id=1, source_target_pairs={{0,8},{8,16},{16,24},{24,32},{32,40},{40,48},{48,56},{56,64},{64,7... | collective-permute-start | bytes 786440 | tf_op jit(solution)/shard_map/ppermute | solution.py:25
  175.3 31.2 %copy-start.11 = (f32[8,4,16,128]{3,0,2,1:T(8,128)}, f32[8,4,16,128]{3,0,2,1:T(8,128)S(1)}, u32[]{:S(2)}) copy-start(f32[8,4,16,128]{3,0,2,1:T(8,128)S(1)} %collective-permute-done.4) | copy-start | bytes 786436
  177.4 29.1 %copy-start.12 = (f32[8,4,16,128]{3,0,2,1:T(8,128)}, f32[8,4,16,128]{3,0,2,1:T(8,128)S(1)}, u32[]{:S(2)}) copy-start(f32[8,4,16,128]{3,0,2,1:T(8,128)S(1)} %collective-permute-done.5) | copy-start | bytes 786436
  177.6 23.2 %collective-permute-start.6 = (f32[8,56,4,128]{3,0,2,1:T(8,128)S(1)}, f32[8,56,4,128]{3,0,2,1:T(8,128)S(1)}, u32[]{:S(2)}, u32[]{:S(2)}) collective-permute-start(f32[8,56,4,128]{3,0,2,1:T(8,128)S(1)} %get-tuple-element.10), channel_id=1, source_target_pairs={{1,0},{2,1},{3,2},{4,3},{5,4},{6,5},{7,6},{0,7},{9,8},{10,9},{11,1... | collective-permute-start | bytes 2752520 | tf_op jit(solution)/shard_map/ppermute | solution.py:26
  183.0 23.5 %collective-permute-start.7 = (f32[8,56,4,128]{3,0,2,1:T(8,128)S(1)}, f32[8,56,4,128]{3,0,2,1:T(8,128)S(1)}, u32[]{:S(2)}, u32[]{:S(2)}) collective-permute-start(f32[8,56,4,128]{3,0,2,1:T(8,128)S(1)} %get-tuple-element.11), channel_id=1, source_target_pairs={{0,1},{1,2},{2,3},{3,4},{4,5},{5,6},{6,7},{7,0},{8,9},{9,10},{10,1... | collective-permute-start | bytes 2752520 | tf_op jit(solution)/shard_map/ppermute | solution.py:25
  190.8 19.6 %copy-start.2 = (f32[8,48,16,128]{3,2,1,0:T(8,128)S(1)}, f32[8,48,16,128]{3,2,1,0:T(8,128)}, u32[]{:S(2)}) copy-start(f32[8,48,16,128]{3,2,1,0:T(8,128)} %param.6) | copy-start | bytes 9437188
  339.6 2.7 copy-start.3
  342.3 6.5 %copy-start.10 = (f32[8,48,16,128]{3,0,2,1:T(8,128)S(1)}, f32[8,48,16,128]{3,0,2,1:T(8,128)}, u32[]{:S(2)}) copy-start(f32[8,48,16,128]{3,0,2,1:T(8,128)} %get-tuple-element.83) | copy-start | bytes 9437188
Sparse Core Ops, SparseCore 0:
  348.9 146.8 all-reduce.1
where the time goes:
time: 528 us; the launch traced here: 519 us
  waiting for transfers between devices  163 us (31%)
  local copies, waits for them, and re-layouts  155 us (29%)
  matrix products  84.6 us (16%)
  blocking collectives  78.8 us (15%)
  starting transfers between devices  17.4 us (3%)
  between operations  15.1 us (3%)
    psum x1, waiting for transfers between devices, on_device(): gram = lax.psum(partial_value, ('grp', 'gx', 'gy'))  145 us
    all_to_all x1, blocking collectives, on_device(): lax.all_to_all(outgoing.reshape(slab_count, capacity, tile_rows, columns)...  78.8 us
    unnamed x53, local copies, waits for them, and re-layouts  72.6 us
    dot_general x2, matrix products, tendency(): jnp.einsum('kj,jxyz->kxyz', reaction, center, precision=lax.Precision.HIG...  63.4 us
    slice x16, local copies, waits for them, and re-layouts, tendency(): jnp.roll(center, offset, 3)  52 us
    ppermute x4, starting transfers between devices, extended(): after = lax.ppermute(initial, axis, down)  13.9 us
    reshape x1, local copies, waits for them, and re-layouts, on_device(): outgoing.reshape(slab_count, capacity, tile_rows, columns)  11.1 us
    convert_element_type x1, local copies, waits for them, and re-layouts, on_device(): outgoing = jnp.einsum('pu,vxuyz->pxvyz', placing, blocks, preferred_eleme...  10.6 us
  transfers between devices with their start and end apart: 9, of which 4 were waited for; matrix products, arithmetic and copies ran while one was open for 20% of the time, Pallas kernels for 0%

commit v1 on v0

--- a/solution.py
+++ b/solution.py
@@ -98,7 +98,7 @@
     partial_value = lax.dot_general(
         received, received, (((0, 2), (0, 2)), ((), ())), preferred_element_type=jnp.float32
     )
-    gram = lax.psum(partial_value, ("grp", "gx", "gy"))
+    gram = lax.psum(lax.psum(partial_value, ("gx", "gy")), "grp")
     product = jnp.dot(gram, start_basis, precision=lax.Precision.HIGHEST)
     basis = product / jnp.sqrt(jnp.sum(product * product))
     for repeat in range(NEWTON):

time: 528 us -> 549 us (1.040)
  waiting for transfers between devices: 163 us -> 184 us
    psum x1 -> x2, waiting for transfers between devices: 145 us -> 166 us  [on_device(): gram = lax.psum(lax.psum(partial_value, ('gx', 'gy')), 'grp')]
  transfers between devices with their start and end apart: 9 -> 10, of which waited for: 4 -> 5; matrix products, arithmetic and copies ran while one was open for 20% -> 19% of each run, Pallas kernels for 0% -> 0%
where the time goes in v1:
time: 549 us; the launch traced here: 540 us
  waiting for transfers between devices  184 us (34%)
  local copies, waits for them, and re-layouts  155 us (28%)
  matrix products  84.4 us (15%)
  blocking collectives  78.9 us (14%)
  starting transfers between devices  17.6 us (3%)
  between operations  15.2 us (3%)
    psum x2, waiting for transfers between devices, on_device(): gram = lax.psum(lax.psum(partial_value, ('gx', 'gy')), 'grp')  166 us
    all_to_all x1, blocking collectives, on_device(): lax.all_to_all(outgoing.reshape(slab_count, capacity, tile_rows, columns)...  78.9 us
    unnamed x53, local copies, waits for them, and re-layouts  72.6 us
    dot_general x2, matrix products, tendency(): jnp.einsum('kj,jxyz->kxyz', reaction, center, precision=lax.Precision.HIG...  63.2 us
    slice x16, local copies, waits for them, and re-layouts, tendency(): jnp.roll(center, offset, 3)  52 us
    ppermute x4, starting transfers between devices, extended(): after = lax.ppermute(initial, axis, down)  13.9 us
    reshape x1, local copies, waits for them, and re-layouts, on_device(): outgoing.reshape(slab_count, capacity, tile_rows, columns)  11.1 us
  transfers between devices with their start and end apart: 10, of which 5 were waited for; matrix products, arithmetic and copies ran while one was open for 19% of the time, Pallas kernels for 0%

profile of v1, /device:TPU:1, one launch (start us, length us, event | category | flops | bytes accessed | tf_op | source)
XLA Modules:
  0.0 540.5 jit_solution(15373320836692329540)
XLA Ops:
  7.2 1.1 fusion.116
  8.3 0.9 copy.103
  9.2 3.0 collective-permute-start.1
  12.2 0.9 copy.104
  13.1 5.8 %fusion.114 = (f32[8,48,16,1]{3,2,1,0:T(8,128)S(1)}, f32[8,48,16,1]{3,2,1,0:T(8,128)}) fusion(f32[8,48,16,128]{3,2,1,0:T(8,128)} %param.6), kind=kLoop, calls=%fused_computation.230 | loop fusion | bytes 98304 | tf_op jit(solution)/shard_map/jit(_roll_static)/slice | solution.py:55
  18.9 3.9 fusion.115
  22.7 1.1 fusion.112
  23.8 3.7 fusion.113
  27.5 1.1 fusion.110
  28.6 1.1 fusion.111
  29.7 1.1 fusion.108
  30.8 1.8 constant_dynamic-update-slice_fusion.3
  32.6 5.7 %constant_dynamic-update-slice_fusion.1 = (f32[8,52,16,128]{3,0,2,1:T(8,128)}, f32[8,52,16,128]{3,0,2,1:T(8,128)}, f32[8,56,16,128]{3,0,2,1:T(8,128)}) fusion(f32[8,48,16,128]{3,2,1,0:T(8,128)S(1)} %copy-done.1, f32[8,52,16,128]{3,0,2,1:T(8,128)} %get-tuple-element.55, f32[8,56,16,128]{3,0,2,1:T(8,128)} %get-tuple-element.56), kind=kLoop, calls=%fused_computation.168 | loop fusion | bytes 12582912
  38.3 0.8 constant_dynamic-update-slice_fusion
  39.2 2.9 fusion.98
  42.0 5.8 %collective-permute-start.2 = (f32[8,56,4,128]{3,0,2,1:T(8,128)}, f32[8,56,4,128]{3,0,2,1:T(8,128)}, u32[]{:S(2)}, u32[]{:S(2)}) collective-permute-start(f32[8,56,4,128]{3,0,2,1:T(8,128)} %get-tuple-element.12), channel_id=1, source_target_pairs={{1,0},{2,1},{3,2},{4,3},{5,4},{6,5},{7,6},{0,7},{9,8},{10,9},{11,1... | collective-permute-start | bytes 2752520 | tf_op jit(solution)/shard_map/ppermute | solution.py:26
  47.9 3.8 fusion.109
  51.7 5.6 %copy.105 = f32[8,48,16,1]{3,0,2,1:T(8,128)} copy(f32[8,48,16,1]{3,2,1,0:T(8,128)} %get-tuple-element.45) | data formatting | bytes 49152
  57.3 3.5 copy.106
  60.8 3.5 copy.107
  64.3 3.5 copy.108
  67.8 3.5 copy.109
  71.4 3.7 copy.110
  75.1 3.4 copy.111
  78.5 3.5 copy.112
  82.0 3.5 copy.113
  85.4 3.4 copy.114
  88.9 3.5 copy.115
  92.4 3.8 copy.116
  96.2 3.5 copy.117
  99.8 3.4 copy.118
  103.2 3.5 copy.119
  106.7 3.4 copy.120
  110.1 0.7 dynamic-slice_bitcast_fusion
  111.0 0.7 multiply_add_fusion
  111.7 37.6 %fusion.43 = f32[8,48,16,128]{3,0,2,1:T(8,128)S(1)} fusion(f32[8,56,16,128]{3,0,2,1:T(8,128)} %get-tuple-element.54, f32[8,56,4,128]{3,0,2,1:T(8,128)} %collective-permute-done.3, f32[8,56,4,128]{3,0,2,1:T(8,128)} %collective-permute-done.2, f32[8,52,16,128]{3,0,2,1:T(8,128)} %get-tuple-element.49, f32[8,52,16,128]{3,0,2,1:T(8,128)} %get-tuple-element.53, ...), kind=kOutput, calls=%fused_computation.70 | convolution fusion | flops 128974848 | bytes 90440736 | tf_op jit(solution)/shard_map/kj,jxyz->kxyz/dot_general | solution.py:40
  149.3 3.8 fusion.99
  153.1 3.8 fusion.100
  157.0 3.8 fusion.101
  160.8 3.9 fusion.102
  164.7 3.8 fusion.103
  168.5 2.8 collective-permute-start.4
  171.2 3.9 fusion.104
  175.1 2.1 collective-permute-done.5
  177.4 5.4 %collective-permute-start.6 = (f32[8,56,4,128]{3,0,2,1:T(8,128)S(1)}, f32[8,56,4,128]{3,0,2,1:T(8,128)S(1)}, u32[]{:S(2)}, u32[]{:S(2)}) collective-permute-start(f32[8,56,4,128]{3,0,2,1:T(8,128)S(1)} %get-tuple-element.10), channel_id=1, source_target_pairs={{1,0},{2,1},{3,2},{4,3},{5,4},{6,5},{7,6},{0,7},{9,8},{10,9},{11,1... | collective-permute-start | bytes 2752520 | tf_op jit(solution)/shard_map/ppermute | solution.py:26
  183.2 3.7 fusion.105
  187.0 3.9 fusion.106
  190.8 9.7 %collective-permute-done.6 = f32[8,56,4,128]{3,0,2,1:T(8,128)S(1)} collective-permute-done((f32[8,56,4,128]{3,0,2,1:T(8,128)S(1)}, f32[8,56,4,128]{3,0,2,1:T(8,128)S(1)}, u32[]{:S(2)}, u32[]{:S(2)}) %collective-permute-start.6) | collective-permute-done | bytes 917536 | tf_op jit(solution)/shard_map/ppermute | solution.py:26
  200.6 5.9 %collective-permute-done.7 = f32[8,56,4,128]{3,0,2,1:T(8,128)S(1)} collective-permute-done((f32[8,56,4,128]{3,0,2,1:T(8,128)S(1)}, f32[8,56,4,128]{3,0,2,1:T(8,128)S(1)}, u32[]{:S(2)}, u32[]{:S(2)}) %collective-permute-start.7) | collective-permute-done | bytes 917536 | tf_op jit(solution)/shard_map/ppermute | solution.py:25
  206.5 3.9 pad_maximum_fusion
  210.4 25.6 %fusion.117 = (bf16[8,48,16,128]{3,0,2,1:T(8,128)(2,1)S(1)}, f32[8,48,16,128]{3,0,2,1:T(8,128)}) fusion(f32[8,48,16,128]{3,0,2,1:T(8,128)S(1)} %fusion.43, f32[8,48,16,124]{3,0,2,1:T(8,128)} %get-tuple-element.16, f32[8,48,16,4]{3,0,2,1:T(8,128)} %get-tuple-element.14, f32[8]{0:T(128)S(1)} %get-tuple-element.62, f32[8,48,16,4]{3,0,2,1:T(8,128)} %get-tuple-element.15, ...), kind=kOutput, calls=%fused_computation.233 | convolution fusion | flops 131334144 | bytes 65028608 | tf_op jit(solution)/shard_map/kj,jxyz->kxyz/dot_general | solution.py:40
  236.0 1.9 convert_bitcast_fusion
  237.9 10.6 %copy.90 = bf16[32,48,8,2,128]{4,3,2,1,0:T(2,128)(2,1)} copy(bf16[32,48,8,2,128]{4,0,3,1,2:T(8,128)(2,1)S(1)} %convert_bitcast_fusion) | data formatting | bytes 12582912 | tf_op jit(solution)/shard_map/convert_element_type | solution.py:89
  248.6 11.1 %reshape.133 = bf16[16,2,48,2048]{3,2,1,0:T(8,128)(2,1)} reshape(bf16[32,48,8,2,128]{4,3,2,1,0:T(2,128)(2,1)} %copy.90) | data formatting | bytes 12582912 | tf_op jit(solution)/shard_map/reshape | solution.py:91
  259.7 78.9 %all_to_all.15 = bf16[16,2,48,2048]{3,2,1,0:T(8,128)(2,1)S(1)} all-to-all(bf16[16,2,48,2048]{3,2,1,0:T(8,128)(2,1)} %reshape.133), channel_id=1, replica_groups=mesh['grp'=4,'gx'=4,'gy'=8] {'grp','gx'}, dimensions={0} | all-to-all | bytes 12582912 | tf_op jit(solution)/shard_map/all_to_all | solution.py:90
  338.6 1.1 copy.91
  339.8 2.7 copy-done.3
  342.4 6.5 %convolution_bitcast_fusion.1 = f32[768,768]{1,0:T(8,128)} fusion(bf16[2,768,2048]{2,1,0:T(8,128)(2,1)S(1)} %bitcast.95), kind=kOutput, calls=%fused_computation.147 | convolution fusion | flops 4831838208 | bytes 8650752 | tf_op jit(solution)/shard_map/dot_general | solution.py:98
  349.0 103.5 %all-reduce.3.cloned.1.call-done = f32[768,768]{1,0:T(8,128)} async-done(((f32[768,768]{1,0:T(8,128)}), f32[768,768]{1,0:T(8,128)}) %all-reduce.3.cloned.1.call-update) | async-done | bytes 2359312 | tf_op jit(solution)/shard_map/psum | solution.py:101
  452.5 2.2 copy.92
  454.8 62.6 %all-reduce.5.cloned.1.call-done = f32[768,768]{1,0:T(8,128)} async-done(((f32[768,768]{1,0:T(8,128)}), f32[768,768]{1,0:T(8,128)}) %all-reduce.5.cloned.1.call-update) | async-done | bytes 2359312 | tf_op jit(solution)/shard_map/psum | solution.py:101
  517.4 4.6 multiply_reduce_fusion
  527.0 4.0 convolution_bitcast_fusion
  530.9 2.5 reshape.135
  (59 shorter events, 5.4 us)
Async XLA Ops:
  7.2 510.2 %copy-start = (f32[768,96]{0,1:T(8,128)S(1)}, f32[768,96]{0,1:T(8,128)}, u32[]{:S(2)}) copy-start(f32[768,96]{0,1:T(8,128)} %param.10) | copy-start | bytes 884740
  7.2 445.3 %all-reduce.3.cloned.1.call-start = ((), (), s32[]{:S(2)}) async-start(), calls=%async_computation.1 | async-start | bytes 4718592 | tf_op jit(solution)/shard_map/psum | solution.py:101
  9.2 21.6 %collective-permute-start.1 = (f32[8,4,16,128]{3,0,2,1:T(8,128)}, f32[8,4,16,128]{3,0,2,1:T(8,128)}, u32[]{:S(2)}, u32[]{:S(2)}) collective-permute-start(f32[8,4,16,128]{3,0,2,1:T(8,128)} %copy.103), channel_id=1, source_target_pairs={{0,8},{8,16},{16,24},{24,32},{32,40},{40,48},{48,56},{56,64},{64,7... | collective-permute-start | bytes 786440 | tf_op jit(solution)/shard_map/ppermute | solution.py:25
  13.1 5.8 %copy-start.1 = (f32[8,48,16,128]{3,2,1,0:T(8,128)S(1)}, f32[8,48,16,128]{3,2,1,0:T(8,128)}, u32[]{:S(2)}) copy-start(f32[8,48,16,128]{3,2,1,0:T(8,128)} %param.6) | copy-start | bytes 9437188
  13.1 25.2 %collective-permute-start = (f32[8,4,16,128]{3,0,2,1:T(8,128)}, f32[8,4,16,128]{3,0,2,1:T(8,128)S(1)}, u32[]{:S(2)}, u32[]{:S(2)}) collective-permute-start(f32[8,4,16,128]{3,0,2,1:T(8,128)} %copy.104), channel_id=1, source_target_pairs={{8,0},{16,8},{24,16},{32,24},{40,32},{48,40},{56,48},{64,56},{72,6... | collective-permute-start | bytes 786440 | tf_op jit(solution)/shard_map/ppermute | solution.py:26
  42.0 69.7 %collective-permute-start.2 = (f32[8,56,4,128]{3,0,2,1:T(8,128)}, f32[8,56,4,128]{3,0,2,1:T(8,128)}, u32[]{:S(2)}, u32[]{:S(2)}) collective-permute-start(f32[8,56,4,128]{3,0,2,1:T(8,128)} %get-tuple-element.12), channel_id=1, source_target_pairs={{1,0},{2,1},{3,2},{4,3},{5,4},{6,5},{7,6},{0,7},{9,8},{10,9},{11,1... | collective-permute-start | bytes 2752520 | tf_op jit(solution)/shard_map/ppermute | solution.py:26
  47.8 63.9 %collective-permute-start.3 = (f32[8,56,4,128]{3,0,2,1:T(8,128)}, f32[8,56,4,128]{3,0,2,1:T(8,128)}, u32[]{:S(2)}, u32[]{:S(2)}) collective-permute-start(f32[8,56,4,128]{3,0,2,1:T(8,128)} %get-tuple-element.13), channel_id=1, source_target_pairs={{0,1},{1,2},{2,3},{3,4},{4,5},{5,6},{6,7},{7,0},{8,9},{9,10},{10,1... | collective-permute-start | bytes 2752520 | tf_op jit(solution)/shard_map/ppermute | solution.py:25
  51.7 5.6 %copy-start.7 = (f32[8,48,16,127]{3,2,1,0:T(8,128)S(1)}, f32[8,48,16,127]{3,2,1,0:T(8,128)}, u32[]{:S(2)}) copy-start(f32[8,48,16,127]{3,2,1,0:T(8,128)} %get-tuple-element.47) | copy-start | bytes 9363460
  57.3 3.5 copy-start.6
  67.8 3.6 copy-start.5
  71.4 3.7 copy-start.4
  96.2 3.5 copy-start.9
  99.7 3.4 copy-start.8
  106.7 4.9 copy-start.13
  106.7 4.9 copy-start.14
  106.7 5.0 copy-start.15
  168.5 6.6 %collective-permute-start.4 = (f32[8,4,16,128]{3,0,2,1:T(8,128)S(1)}, f32[8,4,16,128]{3,0,2,1:T(8,128)S(1)}, u32[]{:S(2)}, u32[]{:S(2)}) collective-permute-start(f32[8,4,16,128]{3,0,2,1:T(8,128)S(1)} %get-tuple-element.30), channel_id=1, source_target_pairs={{8,0},{16,8},{24,16},{32,24},{40,32},{48,40},{56,48},{64,56},{72,6... | collective-permute-start | bytes 786440 | tf_op jit(solution)/shard_map/ppermute | solution.py:26
  171.2 6.0 %collective-permute-start.5 = (f32[8,4,16,128]{3,0,2,1:T(8,128)S(1)}, f32[8,4,16,128]{3,0,2,1:T(8,128)S(1)}, u32[]{:S(2)}, u32[]{:S(2)}) collective-permute-start(f32[8,4,16,128]{3,0,2,1:T(8,128)S(1)} %get-tuple-element.31), channel_id=1, source_target_pairs={{0,8},{8,16},{16,24},{24,32},{32,40},{40,48},{48,56},{56,64},{64,7... | collective-permute-start | bytes 786440 | tf_op jit(solution)/shard_map/ppermute | solution.py:25
  175.1 31.4 %copy-start.11 = (f32[8,4,16,128]{3,0,2,1:T(8,128)}, f32[8,4,16,128]{3,0,2,1:T(8,128)S(1)}, u32[]{:S(2)}) copy-start(f32[8,4,16,128]{3,0,2,1:T(8,128)S(1)} %collective-permute-done.4) | copy-start | bytes 786436
  177.2 29.3 %copy-start.12 = (f32[8,4,16,128]{3,0,2,1:T(8,128)}, f32[8,4,16,128]{3,0,2,1:T(8,128)S(1)}, u32[]{:S(2)}) copy-start(f32[8,4,16,128]{3,0,2,1:T(8,128)S(1)} %collective-permute-done.5) | copy-start | bytes 786436
  177.4 23.2 %collective-permute-start.6 = (f32[8,56,4,128]{3,0,2,1:T(8,128)S(1)}, f32[8,56,4,128]{3,0,2,1:T(8,128)S(1)}, u32[]{:S(2)}, u32[]{:S(2)}) collective-permute-start(f32[8,56,4,128]{3,0,2,1:T(8,128)S(1)} %get-tuple-element.10), channel_id=1, source_target_pairs={{1,0},{2,1},{3,2},{4,3},{5,4},{6,5},{7,6},{0,7},{9,8},{10,9},{11,1... | collective-permute-start | bytes 2752520 | tf_op jit(solution)/shard_map/ppermute | solution.py:26
  182.8 23.7 %collective-permute-start.7 = (f32[8,56,4,128]{3,0,2,1:T(8,128)S(1)}, f32[8,56,4,128]{3,0,2,1:T(8,128)S(1)}, u32[]{:S(2)}, u32[]{:S(2)}) collective-permute-start(f32[8,56,4,128]{3,0,2,1:T(8,128)S(1)} %get-tuple-element.11), channel_id=1, source_target_pairs={{0,1},{1,2},{2,3},{3,4},{4,5},{5,6},{6,7},{7,0},{8,9},{9,10},{10,1... | collective-permute-start | bytes 2752520 | tf_op jit(solution)/shard_map/ppermute | solution.py:25
  190.8 19.6 %copy-start.2 = (f32[8,48,16,128]{3,2,1,0:T(8,128)S(1)}, f32[8,48,16,128]{3,2,1,0:T(8,128)}, u32[]{:S(2)}) copy-start(f32[8,48,16,128]{3,2,1,0:T(8,128)} %param.6) | copy-start | bytes 9437188
  339.8 2.7 copy-start.3
  348.9 103.6 %copy-start.10 = (f32[8,48,16,128]{3,0,2,1:T(8,128)S(1)}, f32[8,48,16,128]{3,0,2,1:T(8,128)}, u32[]{:S(2)}) copy-start(f32[8,48,16,128]{3,0,2,1:T(8,128)} %get-tuple-element.83) | copy-start | bytes 9437188
  349.0 168.4 %all-reduce.5.cloned.1.call-start = ((), (), s32[]{:S(2)}) async-start(), calls=%async_computation.2 | async-start | bytes 4718592 | tf_op jit(solution)/shard_map/psum | solution.py:101
Sparse Core Ops, SparseCore 0:
  349.1 103.3 all-reduce.2
  454.9 62.4 all-reduce.4
